TPU v7x, 256 devices: a whole 4x4x8 slice. The times are simulated.
256 devices in a mesh: ex: 8 (over z_lo, core), ey: 32 (over z_hi, x, y).
Axes of the slice: x: 4, y: 4, z: 8 (z_hi: 2, z_lo: 4; z = z_hi * 4 + z_lo), core: 2. Of those that a mesh axis runs over, the one named last changes fastest.
Arguments:
- tokens: bfloat16 [256, 256, 1024], P(('ex', 'ey')), may hold values from -16 to 16
- slot_param: bfloat16 [1024, 64], replicated, may hold values from -0.75 to 0.75
- weight_in: bfloat16 [64, 1024, 4096], P('ey', None, 'ex'), may hold values from -0.1875 to 0.1875
- weight_out: bfloat16 [64, 4096, 1024], P('ey', 'ex'), may hold values from -0.09375 to 0.09375
- grad_out: bfloat16 [256, 256, 1024], P(('ex', 'ey')), may hold values from -6 to 6
Outputs:
- grad_tokens: bfloat16 [256, 256, 1024], P(('ex', 'ey'))
- grad_param: float32 [1024, 64], replicated
- grad_win: bfloat16 [64, 1024, 4096], P('ey', None, 'ex')
- grad_wout: bfloat16 [64, 4096, 1024], P('ey', 'ex')
All inputs are finite; a program needn't handle non-finite values.
Results may differ from a plain program's by a relative error of at most 0.017.
Values may be sent and summed in bfloat16 or wider, within the bound.
A program may use at most 64 MiB of HBM per device.

v0:
```python
import jax
import jax.numpy as jnp
from jax import lax
from jax.sharding import Mesh
from jax.sharding import PartitionSpec as P

EX = ("ex_0", "ex_1")
EX_EY = ("ex_0", "ex_1", "ey")


def sum_in_order(tiles, axes, sequence):
    inside = tiles.shape[1:]
    tiles = tiles.reshape(*(lax.axis_size(a) for a in axes), *inside)
    tiles = jnp.moveaxis(tiles, sequence, range(len(axes))).reshape(-1, *inside)
    for k in sequence:
        tiles = lax.psum_scatter(tiles, axes[k], scatter_dimension=0, tiled=True)
    return tiles[0]


def in_blocks(array, dim, length):
    before, after = (array.shape[:dim], array.shape[dim + 1 :])
    return jnp.moveaxis(array.reshape(*before, length, -1, *after), dim, 0)


def summed_rows(array, axes, sequence, dim):
    length = lax.axis_size(axes)
    return sum_in_order(in_blocks(array, dim, length), axes, sequence)


def gelu_parts(pre):
    cdf = 0.5 * (1.0 + lax.erf(pre * 0.7071067811865476))
    slope = cdf + pre * jnp.exp(-0.5 * pre * pre) * 0.3989422804014327
    return (pre * cdf, slope)


def softmax_along(values, axis):
    top = jnp.max(values, axis=axis, keepdims=True)
    expo = jnp.exp(values - top)
    return expo / jnp.sum(expo, axis=axis, keepdims=True)


def route_in(stacked):
    moved = lax.all_to_all(stacked, "ey", split_axis=2, concat_axis=0, tiled=True)
    return lax.all_gather(moved, EX, axis=0, tiled=True)


def route_out(term_fn, total_rows):
    summed = summed_rows(
        term_fn(jnp.int32(0), total_rows // lax.axis_size(EX) * lax.axis_size(EX)).astype(
            jnp.bfloat16
        ),
        EX,
        (1, 0),
        0,
    ).astype(jnp.float32)
    return lax.all_to_all(
        summed.astype(jnp.bfloat16), "ey", split_axis=0, concat_axis=2, tiled=True
    )


def per_device(tokens, slot_param, weight_in, weight_out, grad_out):
    logits = jnp.einsum("ipd,ds->ips", tokens, slot_param, preferred_element_type=jnp.float32)
    dispatch = softmax_along(logits, 1)
    combine = softmax_along(logits, 2)
    dispatch_b = dispatch.astype(jnp.bfloat16)
    combine_b = combine.astype(jnp.bfloat16)
    slot_in = jnp.einsum(
        "ips,ipd->isd", dispatch_b, tokens, preferred_element_type=jnp.float32
    ).astype(jnp.bfloat16)
    slot_cot = jnp.einsum(
        "ips,ipd->isd", combine_b, grad_out, preferred_element_type=jnp.float32
    ).astype(jnp.bfloat16)
    arrived = route_in(jnp.stack((slot_in, slot_cot), axis=1))
    total_rows = arrived.shape[0]
    slot_x = arrived[:, 0]
    slot_g = arrived[:, 1]
    pre = jnp.einsum("red,edf->ref", slot_x, weight_in, preferred_element_type=jnp.float32)
    value, slope = gelu_parts(pre)
    hidden = value.astype(jnp.bfloat16)
    back = jnp.einsum("red,efd->ref", slot_g, weight_out, preferred_element_type=jnp.float32)
    dpre = (back * slope).astype(jnp.bfloat16)

    def paired_term(start, count):
        return jnp.concatenate(
            (
                jnp.einsum("ref,efd->red", hidden, weight_out, preferred_element_type=jnp.float32)[
                    :, None
                ],
                jnp.einsum("ref,edf->red", dpre, weight_in, preferred_element_type=jnp.float32)[
                    :, None
                ],
            ),
            axis=1,
        )

    paired = route_out(paired_term, total_rows)
    slot_out = paired[:, 0]
    grad_slot = paired[:, 1]
    grad_win = jnp.einsum("red,ref->edf", slot_x, dpre, preferred_element_type=jnp.float32).astype(
        jnp.bfloat16
    )
    grad_wout = jnp.einsum(
        "ref,red->efd", hidden, slot_g, preferred_element_type=jnp.float32
    ).astype(jnp.bfloat16)
    d_combine = jnp.einsum("ipd,isd->ips", grad_out, slot_out, preferred_element_type=jnp.float32)
    d_dispatch = jnp.einsum("ipd,isd->ips", tokens, grad_slot, preferred_element_type=jnp.float32)
    d_logits = dispatch * (d_dispatch - jnp.sum(dispatch * d_dispatch, axis=1, keepdims=True))
    d_logits = d_logits + combine * (
        d_combine - jnp.sum(combine * d_combine, axis=2, keepdims=True)
    )
    logit_grad = d_logits.astype(jnp.bfloat16)
    grad_tokens = jnp.einsum(
        "ips,isd->ipd", dispatch_b, grad_slot, preferred_element_type=jnp.float32
    )
    grad_tokens = grad_tokens + jnp.einsum(
        "ips,ds->ipd", logit_grad, slot_param, preferred_element_type=jnp.float32
    )
    local_param = jnp.einsum("ipd,ips->ds", tokens, logit_grad, preferred_element_type=jnp.float32)
    grad_param = lax.psum(local_param, EX_EY)
    return (grad_tokens.astype(jnp.bfloat16), grad_param, grad_win, grad_wout)


def solution(mesh):
    split = Mesh(mesh.devices.reshape(4, 2, mesh.shape["ey"]), ("ex_0", "ex_1", "ey"))
    return jax.shard_map(
        per_device,
        mesh=split,
        in_specs=(
            P(EX_EY, None, None),
            P(),
            P("ey", None, EX),
            P("ey", EX, None),
            P(EX_EY, None, None),
        ),
        out_specs=(P(EX_EY, None, None), P(), P("ey", None, EX), P("ey", EX, None)),
        check_vma=False,
    )
```

profile of v0, /device:TPU:2, one launch (start us, length us, event | category | flops | bytes accessed | tf_op | source)
XLA Modules:
  0.0 418.5 jit_solution(196067309297569867)
XLA Ops:
  7.2 0.0 copy-start
  7.2 0.0 all-gather.3.cloned.1.call-start
  7.2 1.6 fusion.34
  8.8 0.2 fusion.23
  9.0 1.3 fusion.4
  10.3 1.2 fusion.5
  11.6 0.3 copy.31
  11.9 25.9 %all_to_all.36 = bf16[1,2,64,1024]{3,1,0,2:T(2,128)(2,1)S(1)} all-to-all(bf16[1,2,64,1024]{3,1,0,2:T(2,128)(2,1)S(1)} %copy.31), channel_id=1, replica_groups=mesh['ex_0'=4,'ex_1'=2,'ey'=32] {'ey'}, dimensions={2} | all-to-all | bytes 524288 | tf_op jit(solution)/shard_map/all_to_all | solution.py:43
  37.8 0.8 copy.59
  38.6 0.0 all-gather.3.cloned.1.call-update
  38.6 0.0 reduce-scatter.3.cloned.1.call-start
  38.7 36.5 %all-gather.3.cloned.1.call-done = bf16[256,1,2,2,1024]{4,0,3,2,1:T(8,128)(2,1)} async-done(((bf16[32,1,2,2,1024]{4,0,3,2,1:T(8,128)(2,1)}), bf16[256,1,2,2,1024]{4,0,3,2,1:T(8,128)(2,1)}) %all-gather.3.cloned.1.call-update) | async-done | bytes 2097168 | tf_op jit(solution)/shard_map/all_gather | solution.py:44
  75.2 2.8 convolution_bitcast_fusion.1
  77.9 0.0 copy-done
  78.0 0.0 copy-done.3
  78.0 1.0 fusion.2
  79.0 0.0 copy-start.5
  79.0 0.0 copy-start.1
  79.0 0.7 convolution_convert_fusion.3
  79.7 1.0 copy-done.1
  80.7 0.7 convolution_convert_fusion.2
  81.5 0.0 copy-done.5
  81.5 0.2 pad_maximum_fusion
  81.7 1.5 copy.41
  83.2 0.0 reduce-scatter.3.cloned.1.call-update
  83.2 0.0 reduce-scatter.5.cloned.1.call-start
  83.3 14.7 %reduce-scatter.3.cloned.1.call-done = bf16[4,32,2,2,1024]{4,1,3,2,0:T(8,128)(2,1)} async-done(((bf16[8,32,2,2,1024]{4,1,3,2,0:T(8,128)(2,1)}), bf16[4,32,2,2,1024]{4,1,3,2,0:T(8,128)(2,1)}) %reduce-scatter.3.cloned.1.call-update) | async-done | bytes 1048592 | tf_op jit(solution)/shard_map/reduce_scatter | solution.py:16
  97.9 0.0 reduce-scatter.5.cloned.1.call-update
  97.9 36.4 %reduce-scatter.5.cloned.1.call-done = bf16[1,32,2,2,1024]{4,1,3,2,0:T(8,128)(2,1)} async-done(((bf16[4,32,2,2,1024]{4,1,3,2,0:T(8,128)(2,1)}), bf16[1,32,2,2,1024]{4,1,3,2,0:T(8,128)(2,1)}) %reduce-scatter.5.cloned.1.call-update) | async-done | bytes 262160 | tf_op jit(solution)/shard_map/reduce_scatter | solution.py:16
  134.4 1.9 copy.35
  136.3 10.2 %all-to-all-start.1 = ((bf16[32,2,2,1024]{3,2,1,0:T(2,128)(2,1)}), bf16[32,2,2,1024]{3,2,1,0:T(2,128)(2,1)S(1)}, u32[]{:S(2)}, u32[]{:S(2)}) async-start(bf16[32,2,2,1024]{3,2,1,0:T(2,128)(2,1)} %copy.35), calls=%async_computation.3 | async-start | bytes 524288 | tf_op jit(solution)/shard_map/all_to_all | solution.py:56
  146.5 0.0 all-reduce.2.cloned.1.call-start
  146.6 3.6 convolution_convert_fusion.1
  150.1 2.1 convolution_convert_fusion
  152.2 6.0 %all-to-all-done.1 = bf16[32,2,2,1024]{3,2,1,0:T(2,128)(2,1)S(1)} async-done(((bf16[32,2,2,1024]{3,2,1,0:T(2,128)(2,1)}), bf16[32,2,2,1024]{3,2,1,0:T(2,128)(2,1)S(1)}, u32[]{:S(2)}, u32[]{:S(2)}) %all-to-all-start.1) | async-done | bytes 262176 | tf_op jit(solution)/shard_map/all_to_all | solution.py:56
  158.3 0.2 copy.36
  158.5 0.4 fusion.35
  158.8 0.0 copy-start.6
  158.9 1.4 convolution_bitcast_fusion.3
  160.2 1.4 fusion.20
  161.6 0.0 copy-done.2
  161.6 0.4 multiply_reduce_fusion.1
  162.0 1.0 convolution_bitcast_fusion.2
  163.0 0.0 all-reduce.2.cloned.1.call-update
  163.0 0.0 copy-done.6
  163.0 2.4 fusion.3
  165.4 244.9 %all-reduce.2.cloned.1.call-done = f32[1024,64]{0,1:T(8,128)} async-done(((f32[1024,64]{0,1:T(8,128)}), f32[1024,64]{0,1:T(8,128)}) %all-reduce.2.cloned.1.call-update) | async-done | bytes 262160 | tf_op jit(solution)/shard_map/psum | solution.py:119
  410.3 1.7 copy.61
  (5 shorter events, 0.0 us)
Async XLA Ops:
  7.2 70.8 %copy-start = (bf16[2,512,1024]{2,1,0:T(8,128)(2,1)S(1)}, bf16[2,512,1024]{2,1,0:T(8,128)(2,1)}, u32[]{:S(2)}) copy-start(bf16[2,512,1024]{2,1,0:T(8,128)(2,1)} %param.8) | copy-start | bytes 6291460
  7.2 68.0 %all-gather.3.cloned.1.call-start = ((), (), s32[]{:S(2)}) async-start(), calls=%async_computation.7 | async-start | bytes 2359296 | tf_op jit(solution)/shard_map/all_gather | solution.py:44
  38.6 59.3 %reduce-scatter.3.cloned.1.call-start = ((), (), s32[]{:S(2)}) async-start(), calls=%async_computation.4 | async-start | bytes 3145728 | tf_op jit(solution)/shard_map/reduce_scatter | solution.py:16
  75.2 2.8 copy-start.3
  79.0 2.5 copy-start.5
  79.0 1.8 copy-start.1
  83.2 51.2 %reduce-scatter.5.cloned.1.call-start = ((), (), s32[]{:S(2)}) async-start(), calls=%async_computation.5 | async-start | bytes 1310720 | tf_op jit(solution)/shard_map/reduce_scatter | solution.py:16
  136.3 21.9 %all-to-all-start.1 = ((bf16[32,2,2,1024]{3,2,1,0:T(2,128)(2,1)}), bf16[32,2,2,1024]{3,2,1,0:T(2,128)(2,1)S(1)}, u32[]{:S(2)}, u32[]{:S(2)}) async-start(bf16[32,2,2,1024]{3,2,1,0:T(2,128)(2,1)} %copy.35), calls=%async_computation.3 | async-start | bytes 524288 | tf_op jit(solution)/shard_map/all_to_all | solution.py:56
  146.5 263.8 %all-reduce.2.cloned.1.call-start = ((), (), s32[]{:S(2)}) async-start(), calls=%async_computation.6 | async-start | bytes 524288 | tf_op jit(solution)/shard_map/psum | solution.py:119
  146.5 3.6 copy-start.4
  152.2 9.4 %copy-start.2 = (bf16[1,256,1024]{2,1,0:T(8,128)(2,1)S(1)}, bf16[1,256,1024]{2,1,0:T(8,128)(2,1)}, u32[]{:S(2)}) copy-start(bf16[1,256,1024]{2,1,0:T(8,128)(2,1)} %param.5) | copy-start | bytes 1572868
  158.8 4.2 copy-start.6
Sparse Core Ops, SparseCore 0:
  38.8 36.3 all-gather.2
  83.3 14.5 reduce-scatter.2
  100.6 33.7 reduce-scatter.4
  163.1 247.1 all-reduce.1
where the time goes:
time: 419 us
  waiting for transfers between devices  339 us (81%)
  blocking collectives  25.9 us (6%)
  matrix products  21.6 us (5%)
  between operations  13.9 us (3%)
  starting transfers between devices  10.3 us (2%)
  local copies, waits for them, and re-layouts  7.79 us (2%)
    psum x1, waiting for transfers between devices, per_device(): grad_param = lax.psum(local_param, EX_EY)  245 us
    reduce_scatter x2, waiting for transfers between devices, sum_in_order(): tiles = lax.psum_scatter(tiles, axes[k], scatter_dimension=0, tiled=True)  51.1 us
    all_gather x1, waiting for transfers between devices, route_in(): return lax.all_gather(moved, EX, axis=0, tiled=True)  36.5 us
    all_to_all x1, blocking collectives, route_in(): lax.all_to_all(stacked, 'ey', split_axis=2, concat_axis=0, tiled=True)  25.9 us
    all_to_all x1, starting transfers between devices, route_out(): lax.all_to_all(summed.astype(jnp.bfloat16), 'ey', split_axis=0, concat_ax...  10.2 us
  transfers between devices with their start and end apart: 5, of which 5 were waited for; matrix products, arithmetic and copies ran while one was open for 2% of the time, Pallas kernels for 0%

commit v1 on v0

--- a/solution.py
+++ b/solution.py
@@ -41,7 +41,7 @@
 
 def route_in(stacked):
     moved = lax.all_to_all(stacked, "ey", split_axis=2, concat_axis=0, tiled=True)
-    return lax.all_gather(moved, EX, axis=0, tiled=True)
+    return jnp.concatenate(lax.all_to_all(jnp.stack([moved] * lax.axis_size(EX)), EX, 0, 0), axis=0)
 
 
 def route_out(term_fn, total_rows):

time: 419 us -> 430 us (1.026)
  blocking collectives: 25.9 us -> 80.2 us
  waiting for transfers between devices: 339 us -> 297 us
    all_to_all x0 -> x1, blocking collectives: none -> 54.3 us  [route_in(): lax.all_to_all(jnp.stack([moved] * lax.axis_size(EX)), EX, 0, 0)]
    all_gather x1 -> x0, waiting for transfers between devices: 36.5 us -> none  [route_in(): return lax.all_gather(moved, EX, axis=0, tiled=True)]
    reduce_scatter x2, waiting for transfers between devices: 51.1 us -> 46 us  [sum_in_order(): tiles = lax.psum_scatter(tiles, axes[k], scatter_dimension=0, tiled=True)]
  transfers between devices with their start and end apart: 5 -> 4, of which waited for: 5 -> 4; matrix products, arithmetic and copies ran while one was open for 2% -> 2% of each run, Pallas kernels for 0% -> 0%
where the time goes in v1:
time: 430 us
  waiting for transfers between devices  297 us (69%)
  blocking collectives  80.2 us (19%)
  matrix products  19.5 us (5%)
  between operations  13.9 us (3%)
  starting transfers between devices  10.3 us (2%)
  local copies, waits for them, and re-layouts  8.67 us (2%)
    psum x1, waiting for transfers between devices, per_device(): grad_param = lax.psum(local_param, EX_EY)  245 us
    all_to_all x1, blocking collectives, route_in(): lax.all_to_all(jnp.stack([moved] * lax.axis_size(EX)), EX, 0, 0)  54.3 us
    reduce_scatter x2, waiting for transfers between devices, sum_in_order(): tiles = lax.psum_scatter(tiles, axes[k], scatter_dimension=0, tiled=True)  46 us
    all_to_all x1, blocking collectives, route_in(): lax.all_to_all(stacked, 'ey', split_axis=2, concat_axis=0, tiled=True)  25.9 us
    all_to_all x1, starting transfers between devices, route_out(): lax.all_to_all(summed.astype(jnp.bfloat16), 'ey', split_axis=0, concat_ax...  10.2 us
  transfers between devices with their start and end apart: 4, of which 4 were waited for; matrix products, arithmetic and copies ran while one was open for 2% of the time, Pallas kernels for 0%

profile of v1, /device:TPU:2, one launch (start us, length us, event | category | flops | bytes accessed | tf_op | source)
XLA Modules:
  0.0 430.0 jit_solution(2312786111298335808)
XLA Ops:
  7.2 0.0 copy-start
  7.2 0.0 reduce-scatter.3.cloned.1.call-start
  7.2 1.6 fusion.34
  8.8 0.2 fusion.23
  9.0 1.3 fusion.4
  10.3 1.2 fusion.5
  11.6 0.3 copy.24
  11.9 25.9 %all_to_all.38 = bf16[1,2,64,1024]{3,1,0,2:T(2,128)(2,1)S(1)} all-to-all(bf16[1,2,64,1024]{3,1,0,2:T(2,128)(2,1)S(1)} %copy.24), channel_id=1, replica_groups=mesh['ex_0'=4,'ex_1'=2,'ey'=32] {'ey'}, dimensions={2} | all-to-all | bytes 524288 | tf_op jit(solution)/shard_map/all_to_all | solution.py:43
  37.8 0.1 copy.25
  37.9 0.3 stack.26
  38.2 54.3 %all_to_all.39 = bf16[8,32,2,2,1024]{4,1,3,2,0:T(8,128)(2,1)S(1)} all-to-all(bf16[8,32,2,2,1024]{4,1,3,2,0:T(8,128)(2,1)S(1)} %stack.26), channel_id=1, replica_groups=mesh['ex_0'=4,'ex_1'=2,'ey'=32] {'ex_0','ex_1'}, dimensions={0} | all-to-all | bytes 4194304 | tf_op jit(solution)/shard_map/all_to_all | solution.py:44
  92.5 0.3 copy.26
  92.7 0.0 copy-start.1
  92.8 2.1 copy-done.3
  94.8 0.7 convolution_bitcast_fusion.1
  95.5 0.0 copy-done.1
  95.5 0.0 copy-done
  95.5 1.0 fusion.2
  96.5 0.0 copy-start.5
  96.5 0.7 convolution_convert_fusion.3
  97.3 0.1 copy-done.5
  97.3 0.7 convolution_convert_fusion.2
  98.1 0.2 pad_maximum_fusion
  98.3 1.5 copy.35
  99.8 0.0 reduce-scatter.3.cloned.1.call-update
  99.8 0.0 reduce-scatter.5.cloned.1.call-start
  99.8 9.5 %reduce-scatter.3.cloned.1.call-done = bf16[4,32,2,2,1024]{4,1,3,2,0:T(8,128)(2,1)} async-done(((bf16[8,32,2,2,1024]{4,1,3,2,0:T(8,128)(2,1)}), bf16[4,32,2,2,1024]{4,1,3,2,0:T(8,128)(2,1)}) %reduce-scatter.3.cloned.1.call-update) | async-done | bytes 1048592 | tf_op jit(solution)/shard_map/reduce_scatter | solution.py:16
  109.4 0.0 reduce-scatter.5.cloned.1.call-update
  109.4 36.4 %reduce-scatter.5.cloned.1.call-done = bf16[1,32,2,2,1024]{4,1,3,2,0:T(8,128)(2,1)} async-done(((bf16[4,32,2,2,1024]{4,1,3,2,0:T(8,128)(2,1)}), bf16[1,32,2,2,1024]{4,1,3,2,0:T(8,128)(2,1)}) %reduce-scatter.5.cloned.1.call-update) | async-done | bytes 262160 | tf_op jit(solution)/shard_map/reduce_scatter | solution.py:16
  145.8 1.9 copy.29
  147.8 10.2 %all-to-all-start.2 = ((bf16[32,2,2,1024]{3,2,1,0:T(2,128)(2,1)}), bf16[32,2,2,1024]{3,2,1,0:T(2,128)(2,1)S(1)}, u32[]{:S(2)}, u32[]{:S(2)}) async-start(bf16[32,2,2,1024]{3,2,1,0:T(2,128)(2,1)} %copy.29), calls=%async_computation.4 | async-start | bytes 524288 | tf_op jit(solution)/shard_map/all_to_all | solution.py:56
  157.9 0.0 all-reduce.2.cloned.1.call-start
  158.0 0.0 copy-start.2
  158.0 3.6 convolution_convert_fusion.1
  161.6 0.0 copy-done.2
  161.6 2.1 convolution_convert_fusion
  163.7 6.0 %all-to-all-done.2 = bf16[32,2,2,1024]{3,2,1,0:T(2,128)(2,1)S(1)} async-done(((bf16[32,2,2,1024]{3,2,1,0:T(2,128)(2,1)}), bf16[32,2,2,1024]{3,2,1,0:T(2,128)(2,1)S(1)}, u32[]{:S(2)}, u32[]{:S(2)}) %all-to-all-start.2) | async-done | bytes 262176 | tf_op jit(solution)/shard_map/all_to_all | solution.py:56
  169.7 0.2 copy.30
  169.9 0.4 fusion.35
  170.3 0.0 copy-start.6
  170.3 1.4 convolution_bitcast_fusion.3
  171.7 1.4 fusion.20
  173.1 0.4 multiply_reduce_fusion.1
  173.5 1.0 convolution_bitcast_fusion.2
  174.4 0.0 all-reduce.2.cloned.1.call-update
  174.5 2.4 fusion.3
  176.9 244.8 %all-reduce.2.cloned.1.call-done = f32[1024,64]{0,1:T(8,128)} async-done(((f32[1024,64]{0,1:T(8,128)}), f32[1024,64]{0,1:T(8,128)}) %all-reduce.2.cloned.1.call-update) | async-done | bytes 262160 | tf_op jit(solution)/shard_map/psum | solution.py:119
  421.8 1.7 copy.53
  (5 shorter events, 0.0 us)
Async XLA Ops:
  7.2 88.4 %copy-start = (bf16[2,512,1024]{2,1,0:T(8,128)(2,1)S(1)}, bf16[2,512,1024]{2,1,0:T(8,128)(2,1)}, u32[]{:S(2)}) copy-start(bf16[2,512,1024]{2,1,0:T(8,128)(2,1)} %param.8) | copy-start | bytes 6291460
  7.2 102.2 %reduce-scatter.3.cloned.1.call-start = ((), (), s32[]{:S(2)}) async-start(), calls=%async_computation.5 | async-start | bytes 3145728 | tf_op jit(solution)/shard_map/reduce_scatter | solution.py:16
  92.5 2.3 copy-start.3
  92.7 2.8 copy-start.1
  96.5 0.8 copy-start.5
  99.8 46.0 %reduce-scatter.5.cloned.1.call-start = ((), (), s32[]{:S(2)}) async-start(), calls=%async_computation.6 | async-start | bytes 1310720 | tf_op jit(solution)/shard_map/reduce_scatter | solution.py:16
  147.8 22.0 %all-to-all-start.2 = ((bf16[32,2,2,1024]{3,2,1,0:T(2,128)(2,1)}), bf16[32,2,2,1024]{3,2,1,0:T(2,128)(2,1)S(1)}, u32[]{:S(2)}, u32[]{:S(2)}) async-start(bf16[32,2,2,1024]{3,2,1,0:T(2,128)(2,1)} %copy.29), calls=%async_computation.4 | async-start | bytes 524288 | tf_op jit(solution)/shard_map/all_to_all | solution.py:56
  157.9 263.8 %all-reduce.2.cloned.1.call-start = ((), (), s32[]{:S(2)}) async-start(), calls=%async_computation.7 | async-start | bytes 524288 | tf_op jit(solution)/shard_map/psum | solution.py:119
  158.0 3.6 copy-start.2
  163.7 9.4 %copy-start.4 = (bf16[1,256,1024]{2,1,0:T(8,128)(2,1)S(1)}, bf16[1,256,1024]{2,1,0:T(8,128)(2,1)}, u32[]{:S(2)}) copy-start(bf16[1,256,1024]{2,1,0:T(8,128)(2,1)} %param.5) | copy-start | bytes 1572868
  170.3 4.2 copy-start.6
Sparse Core Ops, SparseCore 0:
  99.9 9.4 reduce-scatter.2
  112.1 33.7 reduce-scatter.4
  174.6 247.1 all-reduce.1
